TPU v7x, 32 devices: a whole 2x2x4 slice. The times are simulated.
32 devices in a mesh: grp: 2 (over y), ctx: 4 (over z), head: 4 (over x, core).
Axes of the slice: x: 2, y: 2, z: 4, core: 2. Of those that a mesh axis runs over, the one named last changes fastest.
Arguments:
- queries: bfloat16 [16384, 2048], P(('grp', 'ctx', 'head')), parts along dimension 0, may hold values from -6 to 6
- keys: bfloat16 [16384, 2048], P(('grp', 'ctx', 'head')), parts along dimension 0, may hold values from -6 to 6
- values: bfloat16 [16384, 2048], P(('grp', 'ctx', 'head')), parts along dimension 0, may hold values from -6 to 6
- out_grad: bfloat16 [16384, 2048], P(('grp', 'ctx', 'head')), parts along dimension 0, may hold values from -6 to 6
- level_table: float32 [8, 21, 16], P(None, None, 'head'), may hold values from 0.25 to 2
- selector: int32 [256], P(('grp', 'ctx')), parts along dimension 0, may hold values from 0 to 7
Outputs:
- attn_out: bfloat16 [16384, 2048], P(('grp', 'ctx', 'head')), parts along dimension 0
- query_grad: bfloat16 [16384, 2048], P(('grp', 'ctx', 'head')), parts along dimension 0
- key_grad: bfloat16 [16384, 2048], P(('grp', 'ctx', 'head')), parts along dimension 0
- value_grad: bfloat16 [16384, 2048], P(('grp', 'ctx', 'head')), parts along dimension 0
There are 2 independent parts, one for each index of `grp`. A program takes and returns all parts, laid end to end along the dimension named above; an argument that names none is the same for every part. Nothing has to cross between parts.
Inputs may be any that keep to these rules, and one draw needn't show every extreme that they name: `selector`: each stretch's row of the weight table.
All inputs are finite; a program needn't handle non-finite values.
Results may differ from a plain program's by a relative error of at most 0.0051.
Values may be sent and summed in bfloat16 or wider, within the bound.
A program may use at most 256 MiB of HBM per device.

v0:
```python
import math
import jax
import jax.numpy as jnp
from jax import lax
from jax.sharding import PartitionSpec as P

HIGHEST = lax.Precision.HIGHEST


def level_of(xor_value, limit):
    count = jnp.zeros(xor_value.shape, jnp.int32)
    power = 1
    while power < limit:
        count = count + (xor_value >= power).astype(jnp.int32)
        power = power * 2
    return count


def level_weights(level_table, selector, head_width):
    table_rows = jnp.arange(level_table.shape[0], dtype=jnp.int32)
    onehot = (selector[:, None] == table_rows[None, :]).astype(jnp.float32)
    per_stretch = jnp.einsum("cs,slh->clh", onehot, level_table, precision=HIGHEST)
    level_ids = jnp.arange(level_table.shape[1], dtype=jnp.int32).astype(jnp.float32)
    scaling = jnp.exp2(-0.5 * jnp.maximum(level_ids - 1.0, 0.0)) / math.sqrt(head_width)
    return per_stretch * scaling[None, :, None]


def shards(queries, keys, values, out_grad, level_table, selector):
    query_flat, key_flat, value_flat, grad_flat = (
        lax.all_to_all(queries, "head", split_axis=1, concat_axis=0, tiled=True),
        lax.all_to_all(keys, "head", split_axis=1, concat_axis=0, tiled=True),
        lax.all_to_all(values, "head", split_axis=1, concat_axis=0, tiled=True),
        lax.all_to_all(out_grad, "head", split_axis=1, concat_axis=0, tiled=True),
    )
    heads_here = level_table.shape[2]
    tok_count = query_flat.shape[0]
    head_width = query_flat.shape[1] // heads_here
    head_shape = (tok_count, heads_here, head_width)
    query_heads = query_flat.reshape(head_shape)
    key_heads = key_flat.reshape(head_shape)
    value_heads = value_flat.reshape(head_shape)
    grad_heads = grad_flat.reshape(head_shape)
    stretch_count = selector.shape[0]
    stretch_len = tok_count // stretch_count
    per_stretch = level_weights(level_table, selector, head_width)
    lower = tok_count.bit_length() - 1
    token_weights = jnp.repeat(
        jnp.transpose(per_stretch[:, : lower + 1, :], (2, 0, 1)), stretch_len, axis=1
    )
    block_rows = min(512, tok_count)
    positions = jnp.arange(tok_count, dtype=jnp.int32)
    out_parts = []
    query_parts = []
    key_total = jnp.zeros(head_shape, jnp.float32)
    value_total = jnp.zeros(head_shape, jnp.float32)
    for block_index in range(tok_count // block_rows):
        start = block_index * block_rows
        finish = start + block_rows
        query_block = query_heads[start:finish]
        grad_block = grad_heads[start:finish]
        key_part = key_heads[:finish]
        value_part = value_heads[:finish]
        row_pos = positions[start:finish]
        col_pos = positions[:finish]
        level_index = level_of(jnp.bitwise_xor(row_pos[:, None], col_pos[None, :]), tok_count)
        row_weights = token_weights[:, start:finish, :]
        weight = jnp.zeros((heads_here, block_rows, finish), jnp.float32)
        for level_id in range(lower + 1):
            weight = jnp.where(
                (level_index == level_id)[None], row_weights[:, :, level_id][:, :, None], weight
            )
        weight = jnp.where((col_pos[None, :] <= row_pos[:, None])[None], weight, 0.0)
        scores = jnp.einsum(
            "thd,shd->hts", query_block, key_part, preferred_element_type=jnp.float32
        )
        attn_weights = (scores * weight).astype(jnp.bfloat16)
        out_parts.append(
            jnp.einsum("hts,shd->thd", attn_weights, value_part, preferred_element_type=jnp.float32)
        )
        grad_scores = jnp.einsum(
            "thd,shd->hts", grad_block, value_part, preferred_element_type=jnp.float32
        )
        score_grads = (grad_scores * weight).astype(jnp.bfloat16)
        query_parts.append(
            jnp.einsum("hts,shd->thd", score_grads, key_part, preferred_element_type=jnp.float32)
        )
        padding = ((0, tok_count - finish), (0, 0), (0, 0))
        key_total = key_total + jnp.pad(
            jnp.einsum(
                "hts,thd->shd", score_grads, query_block, preferred_element_type=jnp.float32
            ),
            padding,
        )
        value_total = value_total + jnp.pad(
            jnp.einsum(
                "hts,thd->shd", attn_weights, grad_block, preferred_element_type=jnp.float32
            ),
            padding,
        )
    out_local = jnp.concatenate(out_parts, axis=0)
    query_local = jnp.concatenate(query_parts, axis=0)
    stretch_shape = (stretch_count, stretch_len, heads_here, head_width)
    stretch_query = query_heads.reshape(stretch_shape)
    stretch_grad = grad_heads.reshape(stretch_shape)
    block_state = jnp.einsum(
        "shd,she->hde", key_heads, value_heads, preferred_element_type=jnp.float32
    )
    stretch_outer = jnp.einsum(
        "cthd,cthe->chde", stretch_query, stretch_grad, preferred_element_type=jnp.float32
    )
    bits = lax.axis_size("ctx").bit_length() - 1
    cross_weights = per_stretch[:, lower + 1 : lower + 1 + bits, :]
    adjoint_terms = jnp.einsum("cjh,chde->jhde", cross_weights, stretch_outer, precision=HIGHEST)
    position = lax.axis_index("ctx")
    packet = jnp.concatenate([block_state[None], adjoint_terms], axis=0)
    gathered = lax.all_gather(packet, "ctx", axis=0, tiled=True)
    ranks = lax.axis_size("ctx")
    gathered = gathered.reshape(ranks, bits + 1, heads_here, head_width, head_width)
    bit_ids = jnp.arange(bits, dtype=jnp.int32)
    rank_ids = jnp.arange(ranks, dtype=jnp.int32)
    upper_bits = position >> bit_ids & 1
    low_start = position >> bit_ids + 1 << bit_ids + 1
    span_size = jnp.left_shift(jnp.ones_like(bit_ids), bit_ids)
    inside_low = (rank_ids[None, :] >= low_start[:, None]) & (
        rank_ids[None, :] < (low_start + span_size)[:, None]
    )
    inside_high = (rank_ids[None, :] >= (low_start + span_size)[:, None]) & (
        rank_ids[None, :] < (low_start + 2 * span_size)[:, None]
    )
    forward_mask = (inside_low & (upper_bits[:, None] == 1)).astype(jnp.float32)
    backward_mask = (inside_high & (upper_bits[:, None] == 0)).astype(jnp.float32)
    level_stack = jnp.einsum("jn,nhde->jhde", forward_mask, gathered[:, 0], precision=HIGHEST)
    returned = jnp.einsum("jn,njhde->hde", backward_mask, gathered[:, 1:], precision=HIGHEST)
    mixed = jnp.einsum("cjh,jhde->chde", cross_weights, level_stack, precision=HIGHEST).astype(
        jnp.bfloat16
    )
    returned_low = returned.astype(jnp.bfloat16)
    out_cross = jnp.einsum(
        "cthd,chde->cthe", stretch_query, mixed, preferred_element_type=jnp.float32
    ).reshape(head_shape)
    query_cross = jnp.einsum(
        "cthe,chde->cthd", stretch_grad, mixed, preferred_element_type=jnp.float32
    ).reshape(head_shape)
    key_cross = jnp.einsum(
        "she,hde->shd", value_heads, returned_low, preferred_element_type=jnp.float32
    )
    value_cross = jnp.einsum(
        "shd,hde->she", key_heads, returned_low, preferred_element_type=jnp.float32
    )
    flat_shape = (tok_count, heads_here * head_width)
    attn_rows = (out_local + out_cross).astype(jnp.bfloat16).reshape(flat_shape)
    query_rows = (query_local + query_cross).astype(jnp.bfloat16).reshape(flat_shape)
    key_rows = (key_total + key_cross).astype(jnp.bfloat16).reshape(flat_shape)
    value_rows = (value_total + value_cross).astype(jnp.bfloat16).reshape(flat_shape)
    return (
        lax.all_to_all(attn_rows, "head", split_axis=0, concat_axis=1, tiled=True),
        lax.all_to_all(query_rows, "head", split_axis=0, concat_axis=1, tiled=True),
        lax.all_to_all(key_rows, "head", split_axis=0, concat_axis=1, tiled=True),
        lax.all_to_all(value_rows, "head", split_axis=0, concat_axis=1, tiled=True),
    )


def solution(mesh):
    in_specs = (
        P(("grp", "ctx", "head"), None),
        P(("grp", "ctx", "head"), None),
        P(("grp", "ctx", "head"), None),
        P(("grp", "ctx", "head"), None),
        P(None, None, "head"),
        P(("grp", "ctx")),
    )
    out_specs = (
        P(("grp", "ctx", "head"), None),
        P(("grp", "ctx", "head"), None),
        P(("grp", "ctx", "head"), None),
        P(("grp", "ctx", "head"), None),
    )
    return jax.shard_map(shards, mesh=mesh, in_specs=in_specs, out_specs=out_specs, check_vma=False)
```

profile of v0, /device:TPU:0, one launch (start us, length us, event | category | flops | bytes accessed | tf_op | source)
XLA Modules:
  0.0 549.9 jit_solution(6099098687646648184)
XLA Ops:
  19.3 10.5 %broadcast_compare_fusion.24 = (pred[512,1536]{1,0:T(8,128)(4,1)}, pred[512,1536]{1,0:T(8,128)(4,1)}, pred[512,1536]{1,0:T(8,128)(4,1)}, pred[512,1536]{1,0:T(8,...) fusion(s32[1536]{0:T(1024)S(1)} %iota_add_fusion, ...), kind=kLoop, calls=%fused_computation.118 | loop fusion | flops 36175872 | bytes 10231808 | tf_op jit(solution)/shard_map/le | solution.py:72
  29.8 11.2 %all-to-all-done = bf16[512,4,512]{0,2,1:T(8,128)(2,1)S(1)} async-done(((bf16[512,4,512]{0,2,1:T(8,128)(2,1)}), bf16[512,4,512]{0,2,1:T(8,128)(2,1)S(1)}, u32[]{:S(2)}, u32[]{:S(2)}) %all-to-all-start) | async-done | bytes 2097184 | tf_op jit(solution)/shard_map/all_to_all | solution.py:30
  46.0 15.1 %iota_compare_fusion = (pred[512,2048]{1,0:T(8,128)(4,1)}, pred[512,2048]{1,0:T(8,128)(4,1)}, pred[512,2048]{1,0:T(8,128)(4,1)}, pred[512,2048]{1,0:T(8,128)(4,1...) fusion(s32[512]{0:T(512)S(1)} %iota_add_fusion.2), kind=kLoop, calls=%fused_computation.69 | loop fusion | flops 48234496 | bytes 13633536 | tf_op jit(solution)/shard_map/le | solution.py:72
  82.3 19.5 %all-to-all-done.2 = bf16[512,4,512]{2,0,1:T(8,128)(2,1)} async-done(((bf16[512,4,512]{2,0,1:T(8,128)(2,1)}), bf16[512,4,512]{2,0,1:T(8,128)(2,1)}, u32[]{:S(2)}, u32[]{:S(2)}) %all-to-all-start.2) | async-done | bytes 2097184 | tf_op jit(solution)/shard_map/all_to_all | solution.py:32
  106.8 8.4 %broadcast_compare_fusion.37 = (pred[512,1024]{1,0:T(8,128)(4,1)}, pred[512,1024]{1,0:T(8,128)(4,1)}, pred[512,1024]{1,0:T(8,128)(4,1)}, pred[512,1024]{1,0:T(8,...) fusion(s32[1024]{0:T(1024)S(1)} %iota_add_fusion.1, ...), kind=kLoop, calls=%fused_computation.141 | loop fusion | flops 24117248 | bytes 6821888 | tf_op jit(solution)/shard_map/le | solution.py:72
  154.8 5.4 reshape.1384
  177.0 8.1 %multiply_convert_fusion.6 = bf16[4,512,512]{2,1,0:T(8,128)(2,1)S(1)} fusion(bf16[512,4,128]{0,2,1:T(8,128)(2,1)} %bitcast.305, bf16[512,4,128]{0,2,1:T(8,128)(2,1)} %bitcast.298, f32[4,512]{1,0:T(4,128)S(1)} %copy-done.116, f32[4,512]{1,0:T(4,128)} %get-tuple-element.60, f32[4,512]{1,0:T(4,128)} %get-tuple-element.61, f32[4,512]{1,0:T(4,128)} %get-tuple-element.62, ...), kind=kOutput, calls=%fused_computation.53 | convolution fusion | flops 284164096 | bytes 6651904 | tf_op jit(solution)/shard_map/thd,shd->hts/dot_general | solution.py:80
  185.5 6.6 %multiply_convert_fusion.7 = bf16[4,512,512]{2,1,0:T(8,128)(2,1)S(1)} fusion(bf16[512,4,128]{0,2,1:T(8,128)(2,1)S(1)} %bitcast.310, bf16[512,4,128]{0,2,1:T(8,128)(2,1)S(1)} %bitcast.296, f32[4,512]{1,0:T(4,128)S(1)} %copy-done.116, f32[4,512]{1,0:T(4,128)S(1)} %copy-done.117, f32[4,512]{1,0:T(4,128)S(1)} %copy-done.118, f32[4,512]{1,0:T(4,128)S(1)} %copy-done.119, ...), kind=kOutput, calls=%fused_computation.70 | convolution fusion | flops 284164096 | bytes 6651904 | tf_op jit(solution)/shard_map/thd,shd->hts/dot_general | solution.py:73
  196.7 12.1 %multiply_convert_fusion.4 = bf16[4,512,1024]{2,1,0:T(8,128)(2,1)S(1)} fusion(f32[4,512]{1,0:T(4,128)S(1)} %copy-done.103, f32[4,512]{1,0:T(4,128)S(1)} %copy-done.104, f32[4,512]{1,0:T(4,128)S(1)} %copy-done.105, f32[4,512]{1,0:T(4,128)S(1)} %copy-done.106, f32[4,512]{1,0:T(4,128)S(1)} %copy-done.107, f32[4,512]{1,0:T(4,128)S(1)} %copy-done.108, ...), kind=kOutput, calls=%fused_computation.30 | convolution fusion | flops 568328192 | bytes 12681216 | tf_op jit(solution)/shard_map/thd,shd->hts/dot_general | solution.py:80
  208.9 11.5 %multiply_convert_fusion.5 = bf16[4,512,1024]{2,1,0:T(8,128)(2,1)S(1)} fusion(f32[4,512]{1,0:T(4,128)S(1)} %copy-done.103, f32[4,512]{1,0:T(4,128)S(1)} %copy-done.104, f32[4,512]{1,0:T(4,128)S(1)} %copy-done.105, f32[4,512]{1,0:T(4,128)S(1)} %copy-done.106, f32[4,512]{1,0:T(4,128)S(1)} %copy-done.107, f32[4,512]{1,0:T(4,128)S(1)} %copy-done.108, ...), kind=kOutput, calls=%fused_computation.31 | convolution fusion | flops 568328192 | bytes 12681216 | tf_op jit(solution)/shard_map/thd,shd->hts/dot_general | solution.py:73
  226.9 9.5 %fusion.37 = f32[2,4,128,128]{3,0,2,1:T(2,128)S(1)} fusion(f32[32,4,128,128]{3,2,1,0:T(8,128)S(1)} %fusion.28, f32[32,21,4]{0,1,2:T(8,128)S(1)} %convolution_multiply_fusion), kind=kOutput, calls=%fused_computation.124 | convolution fusion | flops 50331648 | bytes 8916992 | tf_op jit(solution)/shard_map/cjh,chde->jhde/dot_general | solution.py:113
  239.0 19.7 %multiply_convert_fusion.2 = bf16[4,512,1536]{2,1,0:T(8,128)(2,1)S(1)} fusion(bf16[512,4,128]{0,2,1:T(8,128)(2,1)S(1)} %bitcast.304, f32[4,512]{1,0:T(4,128)S(1)} %get-tuple-element.33, f32[4,512]{1,0:T(4,128)S(1)} %get-tuple-element.34, f32[4,512]{1,0:T(4,128)S(1)} %get-tuple-element.35, f32[4,512]{1,0:T(4,128)S(1)} %get-tuple-element.36, ...), kind=kOutput, calls=%fused_computation.14 | convolution fusion | flops 852492288 | bytes 18710528 | tf_op jit(solution)/shard_map/thd,shd->hts/dot_general | solution.py:80
  258.9 18.2 %multiply_convert_fusion.3 = bf16[4,512,1536]{2,1,0:T(8,128)(2,1)S(1)} fusion(bf16[512,4,128]{0,2,1:T(8,128)(2,1)S(1)} %bitcast.311, bf16[1536,4,128]{0,2,1:T(8,128)(2,1)S(1)} %copy-done.44, f32[4,512]{1,0:T(4,128)S(1)} %get-tuple-element.33, f32[4,512]{1,0:T(4,128)S(1)} %get-tuple-element.34, f32[4,512]{1,0:T(4,128)S(1)} %get-tuple-element.35, ...), kind=kOutput, calls=%fused_computation.15 | convolution fusion | flops 852492288 | bytes 18710528 | tf_op jit(solution)/shard_map/thd,shd->hts/dot_general | solution.py:73
  283.7 26.3 %multiply_convert_fusion.1 = bf16[4,512,2048]{2,1,0:T(8,128)(2,1)S(1)} fusion(f32[4,512]{1,0:T(4,128)S(1)} %copy-done.89, f32[4,512]{1,0:T(4,128)S(1)} %copy-done.90, f32[4,512]{1,0:T(4,128)S(1)} %copy-done.91, f32[4,512]{1,0:T(4,128)S(1)} %copy-done.92, f32[4,512]{1,0:T(4,128)S(1)} %copy-done.93, f32[4,512]{1,0:T(4,128)S(1)} %copy-done.94, ...), kind=kOutput, calls=%fused_computation.12 | convolution fusion | flops 1136656384 | bytes 24739840 | tf_op jit(solution)/shard_map/thd,shd->hts/dot_general | solution.py:73
  316.7 5.4 copy.213
  322.1 25.2 %multiply_convert_fusion = bf16[4,512,2048]{2,1,0:T(8,128)(2,1)S(1)} fusion(f32[4,512]{1,0:T(4,128)S(1)} %copy-done.89, f32[4,512]{1,0:T(4,128)S(1)} %copy-done.90, f32[4,512]{1,0:T(4,128)S(1)} %copy-done.91, f32[4,512]{1,0:T(4,128)S(1)} %copy-done.92, f32[4,512]{1,0:T(4,128)S(1)} %copy-done.93, f32[4,512]{1,0:T(4,128)S(1)} %copy-done.94, ...), kind=kOutput, calls=%fused_computation.11 | convolution fusion | flops 1136656384 | bytes 24739840 | tf_op jit(solution)/shard_map/thd,shd->hts/dot_general | solution.py:80
  353.8 5.8 %copy.240 = f32[2048,512]{1,0:T(8,128)} copy(f32[2048,512]{0,1:T(8,128)} %pad_maximum_fusion.1) | data formatting | bytes 8388608 | tf_op jit(solution)/shard_map/concatenate | solution.py:101
  364.7 6.8 %convolution_bitcast_fusion.1 = f32[1536,4,128]{2,0,1:T(8,128)} fusion(bf16[4,512,1536]{2,1,0:T(8,128)(2,1)} %copy-done.25, bf16[512,4,128]{0,2,1:T(8,128)(2,1)S(1)} %bitcast.312), kind=kOutput, calls=%fused_computation.77 | convolution fusion | flops 805306368 | bytes 9961472 | tf_op jit(solution)/shard_map/hts,thd->shd/dot_general | solution.py:89
  374.6 7.2 %convert_bitcast_fusion = bf16[32,4,128,128]{3,0,2,1:T(8,128)(2,1)S(1)} fusion(f32[2,4,128,128]{3,0,2,1:T(2,128)S(1)} %fusion.40, f32[32,21,4]{0,1,2:T(8,128)S(1)} %copy-done.88), kind=kOutput, calls=%fused_computation.55 | convolution fusion | flops 52428800 | bytes 4722688 | tf_op jit(solution)/shard_map/cjh,jhde->chde/dot_general | solution.py:134
  386.4 5.5 %copy.243 = f32[32,64,4,128]{3,2,1,0:T(4,128)} copy(f32[32,64,4,128]{3,1,2,0:T(8,128)S(1)} %fusion.22) | data formatting | bytes 8388608 | tf_op jit(solution)/shard_map/cthe,chde->cthd/transpose | solution.py:141
  391.9 5.5 reshape.1375
  397.4 5.5 %add_convert_fusion = bf16[4,512,512]{2,1,0:T(8,128)(2,1)} fusion(f32[4,512,512]{2,1,0:T(8,128)} %bitcast.280, f32[4,512,512]{2,1,0:T(8,128)} %reshape.1375), kind=kLoop, calls=%fused_computation.52 | loop fusion | flops 2097152 | bytes 10485760 | tf_op jit(solution)/shard_map/convert_element_type | solution.py:152
  410.2 8.6 %fusion.69 = f32[4,2048,128]{2,1,0:T(8,128)} fusion(bf16[4,512,2048]{2,1,0:T(8,128)(2,1)} %copy-done.20, bf16[512,4,128]{0,2,1:T(8,128)(2,1)} %bitcast.307), kind=kOutput, calls=%fused_computation.247 | convolution fusion | flops 1073741824 | bytes 13107200 | tf_op jit(solution)/shard_map/hts,thd->shd/dot_general | solution.py:89
  422.9 5.4 fusion.3
  428.3 10.7 %copy.256 = bf16[2048,4,128]{2,1,0:T(4,128)(2,1)} copy(bf16[2048,4,128]{2,0,1:T(8,128)(2,1)S(1)} %fusion.3) | data formatting | bytes 4194304 | tf_op jit(solution)/shard_map/convert_element_type | solution.py:153
  450.7 5.4 convolution_bitcast_fusion.2
  460.3 5.6 %copy.227 = f32[32,64,4,128]{3,2,1,0:T(4,128)} copy(f32[32,64,4,128]{3,1,2,0:T(8,128)S(1)} %fusion.19) | data formatting | bytes 8388608 | tf_op jit(solution)/shard_map/cthd,chde->cthe/transpose | solution.py:138
  465.9 5.5 reshape.1374
  471.4 5.5 %add_convert_fusion.1 = bf16[4,512,512]{2,1,0:T(8,128)(2,1)} fusion(f32[4,512,512]{2,1,0:T(8,128)} %bitcast.279, f32[4,512,512]{2,1,0:T(8,128)} %reshape.1374), kind=kLoop, calls=%fused_computation.54 | loop fusion | flops 2097152 | bytes 10485760 | tf_op jit(solution)/shard_map/convert_element_type | solution.py:151
  481.6 5.2 convolution_bitcast_fusion
  486.9 6.6 %fusion.70 = f32[4,2048,128]{2,1,0:T(8,128)S(1)} fusion(bf16[4,512,2048]{2,1,0:T(8,128)(2,1)} %copy-done.19, bf16[512,4,128]{0,2,1:T(8,128)(2,1)S(1)} %bitcast.302), kind=kOutput, calls=%fused_computation.248 | convolution fusion | flops 1073741824 | bytes 13107200 | tf_op jit(solution)/shard_map/hts,thd->shd/dot_general | solution.py:95
  494.9 9.8 %copy.268 = bf16[2048,4,128]{2,1,0:T(4,128)(2,1)S(1)} copy(bf16[2048,4,128]{2,0,1:T(8,128)(2,1)S(1)} %fusion.2) | data formatting | bytes 4194304 | tf_op jit(solution)/shard_map/convert_element_type | solution.py:154
  (366 shorter events, 216.3 us)
Async XLA Ops:
  7.2 53.9 %copy-start = (f32[8,21,4]{1,2,0:T(4,128)S(1)}, f32[8,21,4]{1,2,0:T(4,128)}, u32[]{:S(2)}) copy-start(f32[8,21,4]{1,2,0:T(4,128)} %param.10) | copy-start | bytes 8068
  11.1 29.9 %all-to-all-start = ((bf16[512,4,512]{0,2,1:T(8,128)(2,1)}), bf16[512,4,512]{0,2,1:T(8,128)(2,1)S(1)}, u32[]{:S(2)}, u32[]{:S(2)}) async-start(bf16[512,4,512]{0,2,1:T(8,128)(2,1)} %bitcast.284), calls=%async_computation | async-start | bytes 4194304 | tf_op jit(solution)/shard_map/all_to_all | solution.py:30
  42.3 29.3 %all-to-all-start.1 = ((bf16[512,4,512]{0,2,1:T(8,128)(2,1)}), bf16[512,4,512]{0,2,1:T(8,128)(2,1)S(1)}, u32[]{:S(2)}, u32[]{:S(2)}) async-start(bf16[512,4,512]{0,2,1:T(8,128)(2,1)} %bitcast.283), calls=%async_computation.1 | async-start | bytes 4194304 | tf_op jit(solution)/shard_map/all_to_all | solution.py:31
  46.0 15.1 %copy-start.132 = (s32[32]{0:T(128)S(1)}, s32[32]{0:T(128)}, u32[]{:S(2)}) copy-start(s32[32]{0:T(128)} %param.11) | copy-start | bytes 388
  61.3 165.5 %copy-start.87 = (f32[32,21,4]{0,1,2:T(8,128)}, f32[32,21,4]{0,1,2:T(8,128)S(1)}, u32[]{:S(2)}) copy-start(f32[32,21,4]{0,1,2:T(8,128)S(1)} %convolution_multiply_fusion) | copy-start | bytes 32260
  71.6 30.2 %all-to-all-start.2 = ((bf16[512,4,512]{2,0,1:T(8,128)(2,1)}), bf16[512,4,512]{2,0,1:T(8,128)(2,1)}, u32[]{:S(2)}, u32[]{:S(2)}) async-start(bf16[512,4,512]{2,0,1:T(8,128)(2,1)} %bitcast.282), calls=%async_computation.2 | async-start | bytes 4194304 | tf_op jit(solution)/shard_map/all_to_all | solution.py:32
  101.8 32.5 %all-to-all-start.3 = ((bf16[512,4,512]{0,2,1:T(8,128)(2,1)}), bf16[512,4,512]{0,2,1:T(8,128)(2,1)}, u32[]{:S(2)}, u32[]{:S(2)}) async-start(bf16[512,4,512]{0,2,1:T(8,128)(2,1)} %bitcast.281), calls=%async_computation.3 | async-start | bytes 4194304 | tf_op jit(solution)/shard_map/all_to_all | solution.py:33
  106.3 265.2 %all-gather.2.cloned.1.call-start = ((), (), s32[]{:S(2)}) async-start(), calls=%async_computation.8 | async-start | bytes 3932160 | tf_op jit(solution)/shard_map/all_gather | solution.py:116
  149.9 12.9 %copy-start.4 = (bf16[2048,4,128]{2,1,0:T(4,128)(2,1)}, bf16[2048,4,128]{2,1,0:T(4,128)(2,1)S(1)}, u32[]{:S(2)}) copy-start(bf16[2048,4,128]{2,1,0:T(4,128)(2,1)S(1)} %reshape.1371) | copy-start | bytes 6291460
  172.4 63.9 %copy-start.6 = (bf16[2048,4,128]{0,2,1:T(8,128)(2,1)}, bf16[2048,4,128]{0,2,1:T(8,128)(2,1)S(1)}, u32[]{:S(2)}) copy-start(bf16[2048,4,128]{0,2,1:T(8,128)(2,1)S(1)} %copy.313) | copy-start | bytes 6291460
  196.7 12.2 %copy-start.27 = (bf16[1024,4,128]{0,2,1:T(8,128)(2,1)S(1)}, bf16[1024,4,128]{0,2,1:T(8,128)(2,1)}, u32[]{:S(2)}) copy-start(bf16[1024,4,128]{0,2,1:T(8,128)(2,1)} %reshape.1383) | copy-start | bytes 3145732
  238.9 19.9 %copy-start.40 = (bf16[1,512,512]{1,2,0:T(8,128)(2,1)S(1)}, bf16[1,512,512]{1,2,0:T(8,128)(2,1)}, u32[]{:S(2)}) copy-start(bf16[1,512,512]{1,2,0:T(8,128)(2,1)} %get-tuple-element.18) | copy-start | bytes 1572868
  238.9 19.9 %copy-start.44 = (bf16[1536,4,128]{0,2,1:T(8,128)(2,1)S(1)}, bf16[1536,4,128]{0,2,1:T(8,128)(2,1)}, u32[]{:S(2)}) copy-start(bf16[1536,4,128]{0,2,1:T(8,128)(2,1)} %reshape.1384) | copy-start | bytes 4718596
  238.9 19.9 %copy-start.50 = (pred[512,1536]{1,0:T(8,128)(4,1)S(1)}, pred[512,1536]{1,0:T(8,128)(4,1)}, u32[]{:S(2)}) copy-start(pred[512,1536]{1,0:T(8,128)(4,1)} %get-tuple-element.68) | copy-start | bytes 2359300
  238.9 19.9 %copy-start.51 = (pred[512,1536]{1,0:T(8,128)(4,1)S(1)}, pred[512,1536]{1,0:T(8,128)(4,1)}, u32[]{:S(2)}) copy-start(pred[512,1536]{1,0:T(8,128)(4,1)} %get-tuple-element.69) | copy-start | bytes 2359300
  238.9 19.9 %copy-start.52 = (pred[512,1536]{1,0:T(8,128)(4,1)S(1)}, pred[512,1536]{1,0:T(8,128)(4,1)}, u32[]{:S(2)}) copy-start(pred[512,1536]{1,0:T(8,128)(4,1)} %get-tuple-element.70) | copy-start | bytes 2359300
  238.9 19.9 %copy-start.53 = (pred[512,1536]{1,0:T(8,128)(4,1)S(1)}, pred[512,1536]{1,0:T(8,128)(4,1)}, u32[]{:S(2)}) copy-start(pred[512,1536]{1,0:T(8,128)(4,1)} %get-tuple-element.71) | copy-start | bytes 2359300
  238.9 19.9 %copy-start.54 = (pred[512,1536]{1,0:T(8,128)(4,1)S(1)}, pred[512,1536]{1,0:T(8,128)(4,1)}, u32[]{:S(2)}) copy-start(pred[512,1536]{1,0:T(8,128)(4,1)} %get-tuple-element.72) | copy-start | bytes 2359300
  238.9 19.9 %copy-start.55 = (pred[512,1536]{1,0:T(8,128)(4,1)S(1)}, pred[512,1536]{1,0:T(8,128)(4,1)}, u32[]{:S(2)}) copy-start(pred[512,1536]{1,0:T(8,128)(4,1)} %get-tuple-element.73) | copy-start | bytes 2359300
  239.0 19.9 %copy-start.56 = (pred[512,1536]{1,0:T(8,128)(4,1)S(1)}, pred[512,1536]{1,0:T(8,128)(4,1)}, u32[]{:S(2)}) copy-start(pred[512,1536]{1,0:T(8,128)(4,1)} %get-tuple-element.74) | copy-start | bytes 2359300
  239.0 19.9 %copy-start.57 = (pred[512,1536]{1,0:T(8,128)(4,1)S(1)}, pred[512,1536]{1,0:T(8,128)(4,1)}, u32[]{:S(2)}) copy-start(pred[512,1536]{1,0:T(8,128)(4,1)} %get-tuple-element.75) | copy-start | bytes 2359300
  239.0 19.9 %copy-start.58 = (pred[512,1536]{1,0:T(8,128)(4,1)S(1)}, pred[512,1536]{1,0:T(8,128)(4,1)}, u32[]{:S(2)}) copy-start(pred[512,1536]{1,0:T(8,128)(4,1)} %get-tuple-element.76) | copy-start | bytes 2359300
  239.0 19.9 %copy-start.59 = (pred[512,1536]{1,0:T(8,128)(4,1)S(1)}, pred[512,1536]{1,0:T(8,128)(4,1)}, u32[]{:S(2)}) copy-start(pred[512,1536]{1,0:T(8,128)(4,1)} %get-tuple-element.77) | copy-start | bytes 2359300
  239.0 19.9 %copy-start.60 = (pred[512,1536]{1,0:T(8,128)(4,1)S(1)}, pred[512,1536]{1,0:T(8,128)(4,1)}, u32[]{:S(2)}) copy-start(pred[512,1536]{1,0:T(8,128)(4,1)} %get-tuple-element.78) | copy-start | bytes 2359300
  239.0 19.9 %copy-start.61 = (pred[512,1536]{1,0:T(8,128)(4,1)S(1)}, pred[512,1536]{1,0:T(8,128)(4,1)}, u32[]{:S(2)}) copy-start(pred[512,1536]{1,0:T(8,128)(4,1)} %get-tuple-element.79) | copy-start | bytes 2359300
  258.8 18.3 %copy-start.25 = (bf16[4,512,1536]{2,1,0:T(8,128)(2,1)}, bf16[4,512,1536]{2,1,0:T(8,128)(2,1)S(1)}, u32[]{:S(2)}) copy-start(bf16[4,512,1536]{2,1,0:T(8,128)(2,1)S(1)} %multiply_convert_fusion.2) | copy-start | bytes 18874372
  283.7 26.4 %copy-start.7 = (bf16[2048,4,128]{0,2,1:T(8,128)(2,1)S(1)}, bf16[2048,4,128]{0,2,1:T(8,128)(2,1)}, u32[]{:S(2)}) copy-start(bf16[2048,4,128]{0,2,1:T(8,128)(2,1)} %copy-done.6) | copy-start | bytes 6291460
  322.1 25.3 %copy-start.22 = (bf16[2048,4,128]{0,2,1:T(8,128)(2,1)S(1)}, bf16[2048,4,128]{0,2,1:T(8,128)(2,1)}, u32[]{:S(2)}) copy-start(bf16[2048,4,128]{0,2,1:T(8,128)(2,1)} %copy.214) | copy-start | bytes 6291460
  402.9 40.2 %all-to-all-start.5 = ((bf16[4,512,512]{2,1,0:T(8,128)(2,1)}), bf16[4,512,512]{2,1,0:T(8,128)(2,1)}, u32[]{:S(2)}, u32[]{:S(2)}) async-start(bf16[4,512,512]{2,1,0:T(8,128)(2,1)} %add_convert_fusion), calls=%async_computation.5 | async-start | bytes 4194304 | tf_op jit(solution)/shard_map/all_to_all | solution.py:157
  443.1 33.7 %all-to-all-start.6 = ((bf16[4,512,512]{2,1,0:T(8,128)(2,1)}), bf16[4,512,512]{2,1,0:T(8,128)(2,1)}, u32[]{:S(2)}, u32[]{:S(2)}) async-start(bf16[4,512,512]{2,1,0:T(8,128)(2,1)} %all_to_all.118), calls=%async_computation.6 | async-start | bytes 4194304 | tf_op jit(solution)/shard_map/all_to_all | solution.py:158
  476.9 30.4 %all-to-all-start.4 = ((bf16[4,512,512]{2,1,0:T(8,128)(2,1)}), bf16[4,512,512]{2,1,0:T(8,128)(2,1)}, u32[]{:S(2)}, u32[]{:S(2)}) async-start(bf16[4,512,512]{2,1,0:T(8,128)(2,1)} %add_convert_fusion.1), calls=%async_computation.4 | async-start | bytes 4194304 | tf_op jit(solution)/shard_map/all_to_all | solution.py:156
  507.3 29.3 %all-to-all-start.7 = ((bf16[4,512,512]{2,1,0:T(8,128)(2,1)}), bf16[4,512,512]{2,1,0:T(8,128)(2,1)S(1)}, u32[]{:S(2)}, u32[]{:S(2)}) async-start(bf16[4,512,512]{2,1,0:T(8,128)(2,1)} %all_to_all.122), calls=%async_computation.7 | async-start | bytes 4194304 | tf_op jit(solution)/shard_map/all_to_all | solution.py:159
  (110 other events, 639.7 us)
Sparse Core Ops, SparseCore 0:
  239.0 66.0 all-gather.1
where the time goes:
time: 559 us; the launch traced here: 550 us
  matrix products  231 us (41%)
  local copies, waits for them, and re-layouts  177 us (32%)
  other arithmetic  56.1 us (10%)
  starting transfers between devices  35.2 us (6%)
  waiting for transfers between devices  33.6 us (6%)
  between operations  16.2 us (3%)
    dot_general x4, matrix products, shards(): jnp.einsum('thd,shd->hts', grad_block, value_part, preferred_element_type...  65.2 us
    dot_general x4, matrix products, shards(): jnp.einsum('thd,shd->hts', query_block, key_part, preferred_element_type=...  62.6 us
    le x4, other arithmetic, shards(): col_pos[None, :] <= row_pos[:, None]  38.2 us
    unnamed x273, local copies, waits for them, and re-layouts  32.9 us
    dot_general x4, matrix products, shards(): jnp.einsum('hts,thd->shd', score_grads, query_block, preferred_element_ty...  23.1 us
    dot_general x4, matrix products, shards(): jnp.einsum('hts,thd->shd', attn_weights, grad_block, preferred_element_ty...  19.8 us
    all_to_all x1, waiting for transfers between devices, shards(): lax.all_to_all(values, 'head', split_axis=1, concat_axis=0, tiled=True)  19.5 us
    slice x7, local copies, waits for them, and re-layouts, shards(): key_part = key_heads[:finish]  17.1 us
  transfers between devices with their start and end apart: 9, of which 5 were waited for; matrix products, arithmetic and copies ran while one was open for 56% of the time, Pallas kernels for 0%

commit v1 on v0

--- a/solution.py
+++ b/solution.py
@@ -1,3 +1,4 @@
+import functools
 import math
 import jax
 import jax.numpy as jnp
@@ -5,6 +6,28 @@
 from jax.sharding import PartitionSpec as P
 
 HIGHEST = lax.Precision.HIGHEST
+
+
+def use_members_all_now(local_x, link_axis):
+    last = lax.psum(1, link_axis)
+    local_part = lax.axis_index(link_axis)
+    arr_next, b_next = (last, local_part)
+    row_out = list(local_x.shape)
+    main = local_x.shape[1] // arr_next
+    row_out[1] = main
+    out_arr = row_out[0]
+    row_out[0] = out_arr * arr_next
+    m_next = jnp.zeros(row_out, local_x.dtype)
+    for b in [*range(arr_next)]:
+        clean = lax.dynamic_slice_in_dim(local_x, (b_next ^ b) * main, main, axis=1)
+        if b:
+            long_array = tuple(((rr, rr ^ b) for rr in range(arr_next)))
+            clean = lax.ppermute(clean, link_axis, long_array)
+        m_next = lax.dynamic_update_slice_in_dim(m_next, clean, (b_next ^ b) * out_arr, axis=0)
+    return m_next
+
+
+lead_circles = functools.partial(use_members_all_now, link_axis="head")
 
 
 def level_of(xor_value, limit):
@@ -29,7 +52,7 @@
     query_flat, key_flat, value_flat, grad_flat = (
         lax.all_to_all(queries, "head", split_axis=1, concat_axis=0, tiled=True),
         lax.all_to_all(keys, "head", split_axis=1, concat_axis=0, tiled=True),
-        lax.all_to_all(values, "head", split_axis=1, concat_axis=0, tiled=True),
+        lead_circles(values),
         lax.all_to_all(out_grad, "head", split_axis=1, concat_axis=0, tiled=True),
     )
     heads_here = level_table.shape[2]

time: 559 us -> 542 us (0.970)
  waiting for transfers between devices: 33.6 us -> 19.9 us
  local copies, waits for them, and re-layouts: 177 us -> 167 us
  matrix products: 231 us -> 238 us
    all_to_all x1 -> x0, waiting for transfers between devices: 19.5 us -> none  [shards(): lax.all_to_all(values, 'head', split_axis=1, concat_axis=0, tiled=True)]
    all_to_all x1, waiting for transfers between devices: 0.84 us -> 12.8 us  [shards(): lax.all_to_all(keys, 'head', split_axis=1, concat_axis=0, tiled=True)]
    all_to_all x1, waiting for transfers between devices: 11.2 us -> 0.01 us  [shards(): lax.all_to_all(queries, 'head', split_axis=1, concat_axis=0, tiled=True)]
    dot_general x4, matrix products: 10.4 us -> 20.5 us  [shards(): jnp.einsum('hts,shd->thd', score_grads, key_part, preferred_element_type=...]
    slice x7 -> x3, local copies, waits for them, and re-layouts: 12.6 us -> 3.31 us  [shards(): value_part = value_heads[:finish]]
    slice x7, local copies, waits for them, and re-layouts: 17.1 us -> 8.47 us  [shards(): key_part = key_heads[:finish]]
    unnamed x273 -> x269, local copies, waits for them, and re-layouts: 32.9 us -> 40.4 us
    reshape x2 -> x0, local copies, waits for them, and re-layouts: 6.94 us -> none  [shards(): value_heads = value_flat.reshape(head_shape)]
  transfers between devices with their start and end apart: 9 -> 11, of which waited for: 5 -> 3; matrix products, arithmetic and copies ran while one was open for 56% -> 51% of each run, Pallas kernels for 0% -> 0%
where the time goes in v1:
time: 542 us; the launch traced here: 532 us
  matrix products  238 us (44%)
  local copies, waits for them, and re-layouts  167 us (31%)
  other arithmetic  58 us (11%)
  starting transfers between devices  33.2 us (6%)
  waiting for transfers between devices  19.9 us (4%)
  between operations  16.2 us (3%)
    dot_general x4, matrix products, shards(): jnp.einsum('thd,shd->hts', grad_block, value_part, preferred_element_type...  68.2 us
    dot_general x4, matrix products, shards(): jnp.einsum('thd,shd->hts', query_block, key_part, preferred_element_type=...  61.5 us
    unnamed x269, local copies, waits for them, and re-layouts  40.4 us
    le x4, other arithmetic, shards(): col_pos[None, :] <= row_pos[:, None]  38.1 us
    dot_general x4, matrix products, shards(): jnp.einsum('hts,shd->thd', score_grads, key_part, preferred_element_type=...  20.5 us
    dot_general x4, matrix products, shards(): jnp.einsum('hts,thd->shd', score_grads, query_block, preferred_element_ty...  19.5 us
    dot_general x4, matrix products, shards(): jnp.einsum('hts,thd->shd', attn_weights, grad_block, preferred_element_ty...  16.5 us
    all_to_all x1, waiting for transfers between devices, shards(): lax.all_to_all(keys, 'head', split_axis=1, concat_axis=0, tiled=True)  12.8 us
  transfers between devices with their start and end apart: 11, of which 3 were waited for; matrix products, arithmetic and copies ran while one was open for 51% of the time, Pallas kernels for 0%

profile of v1, /device:TPU:0, one launch (start us, length us, event | category | flops | bytes accessed | tf_op | source)
XLA Modules:
  0.0 532.4 jit_solution(6454778944967921700)
XLA Ops:
  25.6 15.1 %iota_compare_fusion = (pred[512,2048]{1,0:T(8,128)(4,1)}, pred[512,2048]{1,0:T(8,128)(4,1)}, pred[512,2048]{1,0:T(8,128)(4,1)}, pred[512,2048]{1,0:T(8,128)(4,1...) fusion(s32[512]{0:T(512)S(1)} %iota_add_fusion.2), kind=kLoop, calls=%fused_computation.73 | loop fusion | flops 48234496 | bytes 13633536 | tf_op jit(solution)/shard_map/le | solution.py:95
  40.7 10.5 %broadcast_compare_fusion.24 = (pred[512,1536]{1,0:T(8,128)(4,1)}, pred[512,1536]{1,0:T(8,128)(4,1)}, pred[512,1536]{1,0:T(8,128)(4,1)}, pred[512,1536]{1,0:T(8,...) fusion(s32[1536]{0:T(1024)S(1)} %iota_add_fusion, ...), kind=kLoop, calls=%fused_computation.119 | loop fusion | flops 36175872 | bytes 10231808 | tf_op jit(solution)/shard_map/le | solution.py:95
  72.8 8.3 %broadcast_compare_fusion.37 = (pred[512,1024]{1,0:T(8,128)(4,1)}, pred[512,1024]{1,0:T(8,128)(4,1)}, pred[512,1024]{1,0:T(8,128)(4,1)}, pred[512,1024]{1,0:T(8,...) fusion(s32[1024]{0:T(1024)S(1)} %iota_add_fusion.1, ...), kind=kLoop, calls=%fused_computation.146 | loop fusion | flops 24117248 | bytes 6821888 | tf_op jit(solution)/shard_map/le | solution.py:95
  81.1 12.8 %all-to-all-done.1 = bf16[512,4,512]{0,2,1:T(8,128)(2,1)S(1)} async-done(((bf16[512,4,512]{0,2,1:T(8,128)(2,1)}), bf16[512,4,512]{0,2,1:T(8,128)(2,1)S(1)}, u32[]{:S(2)}, u32[]{:S(2)}) %all-to-all-start.1) | async-done | bytes 2097184 | tf_op jit(solution)/shard_map/all_to_all | solution.py:54
  118.6 5.5 %all-to-all-done.2 = bf16[512,4,512]{0,2,1:T(8,128)(2,1)} async-done(((bf16[512,4,512]{0,2,1:T(8,128)(2,1)}), bf16[512,4,512]{0,2,1:T(8,128)(2,1)}, u32[]{:S(2)}, u32[]{:S(2)}) %all-to-all-start.2) | async-done | bytes 2097184 | tf_op jit(solution)/shard_map/all_to_all | solution.py:56
  133.3 14.2 %fusion.2 = bf16[4,512,1024]{2,1,0:T(8,128)(2,1)} fusion(f32[4,512]{1,0:T(4,128)S(1)} %get-tuple-element.50, f32[4,512]{1,0:T(4,128)S(1)} %get-tuple-element.51, f32[4,512]{1,0:T(4,128)S(1)} %get-tuple-element.52, f32[4,512]{1,0:T(4,128)S(1)} %get-tuple-element.53, f32[4,512]{1,0:T(4,128)S(1)} %get-tuple-element.54, f32[4,512]{1,0:T(4,128)S(1)} %get-tuple-element.55, ...), kind=kOutput, calls=%fused_computation.31 | convolution fusion | flops 568328192 | bytes 12681216 | tf_op jit(solution)/shard_map/thd,shd->hts/dot_general | solution.py:103
  147.6 11.4 %multiply_convert_fusion.2 = bf16[4,512,1024]{2,1,0:T(8,128)(2,1)S(1)} fusion(f32[4,512]{1,0:T(4,128)S(1)} %get-tuple-element.50, f32[4,512]{1,0:T(4,128)S(1)} %get-tuple-element.51, f32[4,512]{1,0:T(4,128)S(1)} %get-tuple-element.52, f32[4,512]{1,0:T(4,128)S(1)} %get-tuple-element.53, f32[4,512]{1,0:T(4,128)S(1)} %get-tuple-element.54, ...), kind=kOutput, calls=%fused_computation.34 | convolution fusion | flops 568328192 | bytes 12681216 | tf_op jit(solution)/shard_map/thd,shd->hts/dot_general | solution.py:96
  169.3 20.4 %fusion.1 = bf16[4,512,1536]{2,1,0:T(8,128)(2,1)} fusion(bf16[1536,4,128]{0,2,1:T(8,128)(2,1)} %bitcast.309, bf16[512,4,128]{0,2,1:T(8,128)(2,1)} %bitcast.334, f32[4,512]{1,0:T(4,128)S(1)} %get-tuple-element.37, f32[4,512]{1,0:T(4,128)S(1)} %get-tuple-element.38, f32[4,512]{1,0:T(4,128)S(1)} %get-tuple-element.39, f32[4,512]{1,0:T(4,128)S(1)} %get-tuple-element.40, ...), kind=kOutput, calls=%fused_computation.16 | convolution fusion | flops 852492288 | bytes 18710528 | tf_op jit(solution)/shard_map/thd,shd->hts/dot_general | solution.py:103
  189.9 17.0 %multiply_convert_fusion.1 = bf16[4,512,1536]{2,1,0:T(8,128)(2,1)S(1)} fusion(bf16[512,4,128]{0,2,1:T(8,128)(2,1)S(1)} %bitcast.326, bf16[1536,4,128]{0,2,1:T(8,128)(2,1)S(1)} %copy-done.41, f32[4,512]{1,0:T(4,128)S(1)} %get-tuple-element.37, f32[4,512]{1,0:T(4,128)S(1)} %get-tuple-element.38, f32[4,512]{1,0:T(4,128)S(1)} %get-tuple-element.39, ...), kind=kOutput, calls=%fused_computation.17 | convolution fusion | flops 852492288 | bytes 18710528 | tf_op jit(solution)/shard_map/thd,shd->hts/dot_general | solution.py:96
  228.7 8.8 %fusion.7 = bf16[4,512,512]{2,1,0:T(8,128)(2,1)} fusion(bf16[512,4,128]{0,2,1:T(8,128)(2,1)} %bitcast.322, bf16[512,4,128]{0,2,1:T(8,128)(2,1)} %bitcast.332, f32[4,512]{1,0:T(4,128)S(1)} %copy-done.100, f32[4,512]{1,0:T(4,128)S(1)} %copy-done.101, f32[4,512]{1,0:T(4,128)S(1)} %copy-done.102, f32[4,512]{1,0:T(4,128)S(1)} %copy-done.103, ...), kind=kOutput, calls=%fused_computation.56 | convolution fusion | flops 284164096 | bytes 6651904 | tf_op jit(solution)/shard_map/thd,shd->hts/dot_general | solution.py:103
  237.6 6.9 %multiply_convert_fusion.3 = bf16[4,512,512]{2,1,0:T(8,128)(2,1)S(1)} fusion(bf16[512,4,128]{0,2,1:T(8,128)(2,1)S(1)} %bitcast.328, bf16[512,4,128]{0,2,1:T(8,128)(2,1)S(1)} %bitcast.321, f32[4,512]{1,0:T(4,128)S(1)} %copy-done.100, f32[4,512]{1,0:T(4,128)S(1)} %copy-done.101, f32[4,512]{1,0:T(4,128)S(1)} %copy-done.102, f32[4,512]{1,0:T(4,128)S(1)} %copy-done.103, ...), kind=kOutput, calls=%fused_computation.74 | convolution fusion | flops 284164096 | bytes 6651904 | tf_op jit(solution)/shard_map/thd,shd->hts/dot_general | solution.py:96
  251.5 9.3 %fusion.42 = f32[2,4,128,128]{3,0,2,1:T(2,128)S(1)} fusion(f32[32,4,128,128]{3,2,1,0:T(8,128)S(1)} %fusion.32, f32[32,21,4]{0,1,2:T(8,128)S(1)} %copy-done.98), kind=kOutput, calls=%fused_computation.128 | convolution fusion | flops 50331648 | bytes 8916992 | tf_op jit(solution)/shard_map/cjh,chde->jhde/dot_general | solution.py:136
  262.5 6.5 %fusion.75 = f32[4,512,128]{1,2,0:T(8,128)} fusion(bf16[4,512,1536]{2,1,0:T(8,128)(2,1)} %fusion.1, bf16[1536,4,128]{0,2,1:T(8,128)(2,1)} %reshape.1378), kind=kOutput, calls=%fused_computation.258 | convolution fusion | flops 805306368 | bytes 8912896 | tf_op jit(solution)/shard_map/hts,shd->thd/dot_general | solution.py:108
  269.1 26.2 %multiply_convert_fusion = bf16[4,512,2048]{2,1,0:T(8,128)(2,1)S(1)} fusion(f32[4,512]{1,0:T(4,128)S(1)} %copy-done.109, f32[4,512]{1,0:T(4,128)S(1)} %copy-done.110, f32[4,512]{1,0:T(4,128)S(1)} %copy-done.111, f32[4,512]{1,0:T(4,128)S(1)} %copy-done.112, f32[4,512]{1,0:T(4,128)S(1)} %copy-done.113, f32[4,512]{1,0:T(4,128)S(1)} %copy-done.114, ...), kind=kOutput, calls=%fused_computation.13 | convolution fusion | flops 1136656384 | bytes 24739840 | tf_op jit(solution)/shard_map/thd,shd->hts/dot_general | solution.py:96
  303.1 5.6 %copy.218 = f32[2048,512]{1,0:T(8,128)} copy(f32[2048,512]{0,1:T(8,128)} %pad_maximum_fusion) | data formatting | bytes 8388608 | tf_op jit(solution)/shard_map/concatenate | solution.py:123
  308.9 8.7 %fusion.77 = f32[4,2048,128]{2,1,0:T(8,128)} fusion(bf16[4,512,2048]{2,1,0:T(8,128)(2,1)} %copy-done.2, bf16[512,4,128]{0,2,1:T(8,128)(2,1)} %bitcast.330), kind=kOutput, calls=%fused_computation.260 | convolution fusion | flops 1073741824 | bytes 13107200 | tf_op jit(solution)/shard_map/hts,thd->shd/dot_general | solution.py:118
  317.7 24.8 %fusion = bf16[4,512,2048]{2,1,0:T(8,128)(2,1)} fusion(f32[4,512]{1,0:T(4,128)S(1)} %copy-done.109, f32[4,512]{1,0:T(4,128)S(1)} %copy-done.110, f32[4,512]{1,0:T(4,128)S(1)} %copy-done.111, f32[4,512]{1,0:T(4,128)S(1)} %copy-done.112, f32[4,512]{1,0:T(4,128)S(1)} %copy-done.113, f32[4,512]{1,0:T(4,128)S(1)} %copy-done.114, f32[4,512]{1,0:T(4,128)S(1)} %copy-done.115, ...), kind=kOutput, calls=%fused_computation.12 | convolution fusion | flops 1136656384 | bytes 24739840 | tf_op jit(solution)/shard_map/thd,shd->hts/dot_general | solution.py:103
  345.5 7.4 %convert_bitcast_fusion = bf16[32,4,128,128]{3,0,2,1:T(8,128)(2,1)S(1)} fusion(f32[2,4,128,128]{3,0,2,1:T(2,128)S(1)} %fusion.48, f32[32,21,4]{0,1,2:T(8,128)S(1)} %copy-done.98), kind=kOutput, calls=%fused_computation.59 | convolution fusion | flops 52428800 | bytes 4722688 | tf_op jit(solution)/shard_map/cjh,jhde->chde/dot_general | solution.py:157
  359.2 5.6 %copy.231 = f32[32,64,4,128]{3,2,1,0:T(4,128)} copy(f32[32,64,4,128]{3,1,2,0:T(8,128)S(1)} %fusion.23) | data formatting | bytes 8388608 | tf_op jit(solution)/shard_map/cthd,chde->cthe/transpose | solution.py:161
  364.8 5.5 %reshape.1370 = f32[4,512,512]{2,1,0:T(8,128)} reshape(f32[32,64,4,128]{3,2,1,0:T(4,128)} %copy.231) | data formatting | bytes 8388608 | tf_op jit(solution)/shard_map/reshape | solution.py:163
  370.2 5.5 %add_convert_fusion.1 = bf16[4,512,512]{2,1,0:T(8,128)(2,1)} fusion(f32[4,512,512]{2,1,0:T(8,128)} %bitcast.298, f32[4,512,512]{2,1,0:T(8,128)} %reshape.1370), kind=kLoop, calls=%fused_computation.58 | loop fusion | flops 2097152 | bytes 10485760 | tf_op jit(solution)/shard_map/convert_element_type | solution.py:174
  383.9 8.0 %fusion.36 = f32[4,512,128]{1,2,0:T(8,128)} fusion(bf16[4,512,2048]{2,1,0:T(8,128)(2,1)} %fusion, bf16[2048,4,128]{2,1,0:T(4,128)(2,1)} %reshape.1368), kind=kOutput, calls=%fused_computation.122 | convolution fusion | flops 1073741824 | bytes 11534336 | tf_op jit(solution)/shard_map/hts,shd->thd/dot_general | solution.py:108
  395.9 5.2 fusion.5
  401.2 10.7 %copy.276 = bf16[2048,4,128]{2,1,0:T(4,128)(2,1)} copy(bf16[2048,4,128]{2,0,1:T(8,128)(2,1)S(1)} %fusion.5) | data formatting | bytes 4194304 | tf_op jit(solution)/shard_map/convert_element_type | solution.py:177
  425.1 5.5 %copy.248 = f32[2048,512]{1,0:T(8,128)} copy(f32[2048,512]{0,1:T(8,128)} %pad_maximum_fusion.1) | data formatting | bytes 8388608 | tf_op jit(solution)/shard_map/concatenate | solution.py:124
  430.6 5.3 convolution_bitcast_fusion.3
  440.4 5.6 %copy.251 = f32[32,64,4,128]{3,2,1,0:T(4,128)} copy(f32[32,64,4,128]{3,1,2,0:T(8,128)S(1)} %fusion.26) | data formatting | bytes 8388608 | tf_op jit(solution)/shard_map/cthe,chde->cthd/transpose | solution.py:164
  446.0 5.5 %reshape.1371 = f32[4,512,512]{2,1,0:T(8,128)} reshape(f32[32,64,4,128]{3,2,1,0:T(4,128)} %copy.251) | data formatting | bytes 8388608 | tf_op jit(solution)/shard_map/reshape | solution.py:166
  451.5 5.5 %add_convert_fusion = bf16[4,512,512]{2,1,0:T(8,128)(2,1)} fusion(f32[4,512,512]{2,1,0:T(8,128)} %bitcast.299, f32[4,512,512]{2,1,0:T(8,128)} %reshape.1371), kind=kLoop, calls=%fused_computation.57 | loop fusion | flops 2097152 | bytes 10485760 | tf_op jit(solution)/shard_map/convert_element_type | solution.py:175
  464.5 5.2 convolution_bitcast_fusion.1
  469.7 6.6 %fusion.76 = f32[4,2048,128]{2,1,0:T(8,128)S(1)} fusion(bf16[4,512,2048]{2,1,0:T(8,128)(2,1)} %fusion, bf16[512,4,128]{0,2,1:T(8,128)(2,1)S(1)} %bitcast.325), kind=kOutput, calls=%fused_computation.259 | convolution fusion | flops 1073741824 | bytes 13107200 | tf_op jit(solution)/shard_map/hts,thd->shd/dot_general | solution.py:112
  477.7 9.9 %copy.264 = bf16[2048,4,128]{2,1,0:T(4,128)(2,1)S(1)} copy(bf16[2048,4,128]{2,0,1:T(8,128)(2,1)S(1)} %fusion.6) | data formatting | bytes 4194304 | tf_op jit(solution)/shard_map/convert_element_type | solution.py:176
  (365 shorter events, 207.3 us)
Async XLA Ops:
  7.2 44.1 %copy-start = (f32[8,21,4]{1,2,0:T(4,128)S(1)}, f32[8,21,4]{1,2,0:T(4,128)}, u32[]{:S(2)}) copy-start(f32[8,21,4]{1,2,0:T(4,128)} %param.10) | copy-start | bytes 8068
  11.1 51.8 %all-to-all-start = ((bf16[512,4,512]{0,2,1:T(8,128)(2,1)}), bf16[512,4,512]{0,2,1:T(8,128)(2,1)S(1)}, u32[]{:S(2)}, u32[]{:S(2)}) async-start(bf16[512,4,512]{0,2,1:T(8,128)(2,1)} %bitcast.300), calls=%async_computation | async-start | bytes 4194304 | tf_op jit(solution)/shard_map/all_to_all | solution.py:53
  20.1 81.7 %collective-permute-start = (bf16[512,512]{0,1:T(8,128)(2,1)}, bf16[512,512]{0,1:T(8,128)(2,1)}, u32[]{:S(2)}, u32[]{:S(2)}) collective-permute-start(bf16[512,512]{0,1:T(8,128)(2,1)} %copy.325), channel_id=1, source_target_pairs={{0,1},{1,0},{2,3},{3,2},{4,5},{5,4},{6,7},{7,6},{8,9},{9,8},{10,11... | collective-permute-start | bytes 1572872 | tf_op jit(solution)/shard_map/ppermute | solution.py:25
  22.6 80.3 %collective-permute-start.1 = (bf16[512,512]{0,1:T(8,128)(2,1)}, bf16[512,512]{0,1:T(8,128)(2,1)}, u32[]{:S(2)}, u32[]{:S(2)}) collective-permute-start(bf16[512,512]{0,1:T(8,128)(2,1)} %copy.326), channel_id=1, source_target_pairs={{0,2},{1,3},{2,0},{3,1},{4,6},{5,7},{6,4},{7,5},{8,10},{9,11},{10,... | collective-permute-start | bytes 1572872 | tf_op jit(solution)/shard_map/ppermute | solution.py:25
  25.5 78.5 %collective-permute-start.2 = (bf16[512,512]{0,1:T(8,128)(2,1)}, bf16[512,512]{0,1:T(8,128)(2,1)}, u32[]{:S(2)}, u32[]{:S(2)}) collective-permute-start(bf16[512,512]{0,1:T(8,128)(2,1)} %copy.327), channel_id=1, source_target_pairs={{0,3},{1,2},{2,1},{3,0},{4,7},{5,6},{6,5},{7,4},{8,11},{9,10},{10,... | collective-permute-start | bytes 1572872 | tf_op jit(solution)/shard_map/ppermute | solution.py:25
  64.2 29.7 %all-to-all-start.1 = ((bf16[512,4,512]{0,2,1:T(8,128)(2,1)}), bf16[512,4,512]{0,2,1:T(8,128)(2,1)S(1)}, u32[]{:S(2)}, u32[]{:S(2)}) async-start(bf16[512,4,512]{0,2,1:T(8,128)(2,1)} %bitcast.302), calls=%async_computation.1 | async-start | bytes 4194304 | tf_op jit(solution)/shard_map/all_to_all | solution.py:54
  93.9 30.2 %all-to-all-start.2 = ((bf16[512,4,512]{0,2,1:T(8,128)(2,1)}), bf16[512,4,512]{0,2,1:T(8,128)(2,1)}, u32[]{:S(2)}, u32[]{:S(2)}) async-start(bf16[512,4,512]{0,2,1:T(8,128)(2,1)} %bitcast.301), calls=%async_computation.2 | async-start | bytes 4194304 | tf_op jit(solution)/shard_map/all_to_all | solution.py:56
  98.4 244.0 %all-gather.2.cloned.1.call-start = ((), (), s32[]{:S(2)}) async-start(), calls=%async_computation.7 | async-start | bytes 3932160 | tf_op jit(solution)/shard_map/all_gather | solution.py:139
  133.2 14.3 %copy-start.38 = (bf16[1,512,512]{1,2,0:T(8,128)(2,1)S(1)}, bf16[1,512,512]{1,2,0:T(8,128)(2,1)}, u32[]{:S(2)}) copy-start(bf16[1,512,512]{1,2,0:T(8,128)(2,1)} %get-tuple-element.19) | copy-start | bytes 1572868
  169.2 20.6 %copy-start.31 = (bf16[1,512,512]{1,2,0:T(8,128)(2,1)S(1)}, bf16[1,512,512]{1,2,0:T(8,128)(2,1)}, u32[]{:S(2)}) copy-start(bf16[1,512,512]{1,2,0:T(8,128)(2,1)} %get-tuple-element.18) | copy-start | bytes 1572868
  169.2 20.6 %copy-start.41 = (bf16[1536,4,128]{0,2,1:T(8,128)(2,1)S(1)}, bf16[1536,4,128]{0,2,1:T(8,128)(2,1)}, u32[]{:S(2)}) copy-start(bf16[1536,4,128]{0,2,1:T(8,128)(2,1)} %reshape.1378) | copy-start | bytes 4718596
  169.2 20.6 %copy-start.58 = (pred[512,1536]{1,0:T(8,128)(4,1)S(1)}, pred[512,1536]{1,0:T(8,128)(4,1)}, u32[]{:S(2)}) copy-start(pred[512,1536]{1,0:T(8,128)(4,1)} %get-tuple-element.72) | copy-start | bytes 2359300
  169.2 20.6 %copy-start.59 = (pred[512,1536]{1,0:T(8,128)(4,1)S(1)}, pred[512,1536]{1,0:T(8,128)(4,1)}, u32[]{:S(2)}) copy-start(pred[512,1536]{1,0:T(8,128)(4,1)} %get-tuple-element.73) | copy-start | bytes 2359300
  169.2 20.6 %copy-start.60 = (pred[512,1536]{1,0:T(8,128)(4,1)S(1)}, pred[512,1536]{1,0:T(8,128)(4,1)}, u32[]{:S(2)}) copy-start(pred[512,1536]{1,0:T(8,128)(4,1)} %get-tuple-element.74) | copy-start | bytes 2359300
  169.2 20.6 %copy-start.61 = (pred[512,1536]{1,0:T(8,128)(4,1)S(1)}, pred[512,1536]{1,0:T(8,128)(4,1)}, u32[]{:S(2)}) copy-start(pred[512,1536]{1,0:T(8,128)(4,1)} %get-tuple-element.75) | copy-start | bytes 2359300
  169.2 20.6 %copy-start.62 = (pred[512,1536]{1,0:T(8,128)(4,1)S(1)}, pred[512,1536]{1,0:T(8,128)(4,1)}, u32[]{:S(2)}) copy-start(pred[512,1536]{1,0:T(8,128)(4,1)} %get-tuple-element.76) | copy-start | bytes 2359300
  169.2 20.6 %copy-start.63 = (pred[512,1536]{1,0:T(8,128)(4,1)S(1)}, pred[512,1536]{1,0:T(8,128)(4,1)}, u32[]{:S(2)}) copy-start(pred[512,1536]{1,0:T(8,128)(4,1)} %get-tuple-element.77) | copy-start | bytes 2359300
  169.2 20.6 %copy-start.64 = (pred[512,1536]{1,0:T(8,128)(4,1)S(1)}, pred[512,1536]{1,0:T(8,128)(4,1)}, u32[]{:S(2)}) copy-start(pred[512,1536]{1,0:T(8,128)(4,1)} %get-tuple-element.78) | copy-start | bytes 2359300
  169.2 20.6 %copy-start.65 = (pred[512,1536]{1,0:T(8,128)(4,1)S(1)}, pred[512,1536]{1,0:T(8,128)(4,1)}, u32[]{:S(2)}) copy-start(pred[512,1536]{1,0:T(8,128)(4,1)} %get-tuple-element.79) | copy-start | bytes 2359300
  169.2 20.6 %copy-start.66 = (pred[512,1536]{1,0:T(8,128)(4,1)S(1)}, pred[512,1536]{1,0:T(8,128)(4,1)}, u32[]{:S(2)}) copy-start(pred[512,1536]{1,0:T(8,128)(4,1)} %get-tuple-element.80) | copy-start | bytes 2359300
  169.2 20.6 %copy-start.67 = (pred[512,1536]{1,0:T(8,128)(4,1)S(1)}, pred[512,1536]{1,0:T(8,128)(4,1)}, u32[]{:S(2)}) copy-start(pred[512,1536]{1,0:T(8,128)(4,1)} %get-tuple-element.81) | copy-start | bytes 2359300
  169.2 20.6 %copy-start.68 = (pred[512,1536]{1,0:T(8,128)(4,1)S(1)}, pred[512,1536]{1,0:T(8,128)(4,1)}, u32[]{:S(2)}) copy-start(pred[512,1536]{1,0:T(8,128)(4,1)} %get-tuple-element.82) | copy-start | bytes 2359300
  169.3 20.6 %copy-start.69 = (pred[512,1536]{1,0:T(8,128)(4,1)S(1)}, pred[512,1536]{1,0:T(8,128)(4,1)}, u32[]{:S(2)}) copy-start(pred[512,1536]{1,0:T(8,128)(4,1)} %get-tuple-element.83) | copy-start | bytes 2359300
  169.3 20.6 %copy-start.70 = (pred[512,1536]{1,0:T(8,128)(4,1)S(1)}, pred[512,1536]{1,0:T(8,128)(4,1)}, u32[]{:S(2)}) copy-start(pred[512,1536]{1,0:T(8,128)(4,1)} %get-tuple-element.84) | copy-start | bytes 2359300
  189.9 17.0 %copy-start.20 = (bf16[1536,512]{0,1:T(8,128)(2,1)S(1)}, bf16[1536,512]{0,1:T(8,128)(2,1)}, u32[]{:S(2)}) copy-start(bf16[1536,512]{0,1:T(8,128)(2,1)} %slice.572) | copy-start | bytes 4718596
  317.6 26.1 %copy-start.125 = (s32[2]{0:T(128)S(1)}, s32[2]{0:T(128)}, u32[]{:S(2)}) copy-start(s32[2]{0:T(128)} %copy-done.124) | copy-start | bytes 28
  317.6 26.1 %copy-start.126 = (pred[2]{0:T(512)(128)(4,1)S(1)}, pred[2]{0:T(512)(128)(4,1)}, u32[]{:S(2)}) copy-start(pred[2]{0:T(512)(128)(4,1)} %get-tuple-element.127) | copy-start | bytes 10
  317.6 26.1 %copy-start.127 = (s32[2]{0:T(128)S(1)}, s32[2]{0:T(128)}, u32[]{:S(2)}) copy-start(s32[2]{0:T(128)} %get-tuple-element.124) | copy-start | bytes 28
  375.7 40.4 %all-to-all-start.3 = ((bf16[4,512,512]{2,1,0:T(8,128)(2,1)}), bf16[4,512,512]{2,1,0:T(8,128)(2,1)}, u32[]{:S(2)}, u32[]{:S(2)}) async-start(bf16[4,512,512]{2,1,0:T(8,128)(2,1)} %add_convert_fusion.1), calls=%async_computation.3 | async-start | bytes 4194304 | tf_op jit(solution)/shard_map/all_to_all | solution.py:179
  416.1 40.9 %all-to-all-start.6 = ((bf16[4,512,512]{2,1,0:T(8,128)(2,1)}), bf16[4,512,512]{2,1,0:T(8,128)(2,1)}, u32[]{:S(2)}, u32[]{:S(2)}) async-start(bf16[4,512,512]{2,1,0:T(8,128)(2,1)} %all_to_all.107), calls=%async_computation.6 | async-start | bytes 4194304 | tf_op jit(solution)/shard_map/all_to_all | solution.py:182
  457.0 32.8 %all-to-all-start.4 = ((bf16[4,512,512]{2,1,0:T(8,128)(2,1)}), bf16[4,512,512]{2,1,0:T(8,128)(2,1)}, u32[]{:S(2)}, u32[]{:S(2)}) async-start(bf16[4,512,512]{2,1,0:T(8,128)(2,1)} %add_convert_fusion), calls=%async_computation.4 | async-start | bytes 4194304 | tf_op jit(solution)/shard_map/all_to_all | solution.py:180
  489.8 29.3 %all-to-all-start.5 = ((bf16[4,512,512]{2,1,0:T(8,128)(2,1)}), bf16[4,512,512]{2,1,0:T(8,128)(2,1)S(1)}, u32[]{:S(2)}, u32[]{:S(2)}) async-start(bf16[4,512,512]{2,1,0:T(8,128)(2,1)} %all_to_all.103), calls=%async_computation.5 | async-start | bytes 4194304 | tf_op jit(solution)/shard_map/all_to_all | solution.py:181
  (108 other events, 824.6 us)
Sparse Core Ops, SparseCore 0:
  262.4 64.3 all-gather.1
